TPU v7x, 128 devices: a whole 4x4x4 slice. The times are simulated.
128 devices in a mesh: dp: 8 (over x, core), seq: 16 (over y, z).
Axes of the slice: x: 4, y: 4, z: 4, core: 2. Of those that a mesh axis runs over, the one named last changes fastest.
Arguments:
- candidates: bfloat16 [32768, 256], P(('dp', 'seq')), may hold values from -6 to 6
- scenarios: int32 [32768], P(('dp', 'seq')), may hold values from 0 to 15
- candidate_user: int32 [32768], P(('dp', 'seq')), may hold values from 0 to 15, as said below
- gate_table: float32 [16, 256], replicated, may hold values from 0.1 to 1.9
- log_normalizer: float32 [32768], P(('dp', 'seq')), as said below
- forward_out: bfloat16 [32768, 256], P(('dp', 'seq')), may hold values from -1.5 to 1.5
- out_grad: bfloat16 [32768, 256], P(('dp', 'seq')), may hold values from -96 to 96
- history: bfloat16 [16, 8192, 256], P('dp', 'seq'), may hold values from -6 to 6
- history_length: int32 [16], P('dp'), may hold values from 1024 to 8192, as said below
- history_items: int32 [16, 8192], P('dp', 'seq'), may hold values from 0 to 524287, as said below
Outputs:
- candidate_grad: float32 [32768, 256], P(('dp', 'seq'))
- table_grad: float32 [524288, 256], P(('dp', 'seq'))
Inputs may be any that keep to these rules, and one draw needn't show every extreme that they name: `candidate_user`: candidate c belongs to one of the 2 users numbered from (c // (256 * 16)) * 2; all 256 candidates held by one device belong to the same user, and each of those 2 users owns the candidates of exactly 16 // 2 of the group's devices. `history_length`: every user has at least 1024 valid positions; some user has all 8192. `log_normalizer`: within 1.5 of 0.5 plus the log of the length of the candidate's user. `history_items`: the table rows k * 4096 to (k + 1) * 4096 - 1 are owner k's; of the history positions held by one device, at most 16 name rows of one owner, and in every draw some owner is named by exactly 16 positions of every device.
All inputs are finite; a program needn't handle non-finite values.
Results may differ from a plain program's by a relative error of at most 0.0045.
Values may be sent and summed in bfloat16 or wider, within the bound.
A program may use at most 64 MiB of HBM per device.

v0:
```python
import math

import jax
import jax.numpy as jnp
from jax import lax
from jax.experimental import pallas as pl
from jax.experimental.pallas import tpu as pltpu
from jax.sharding import PartitionSpec as P

ITEM_DEV = 4096
MESH = pl.DeviceIdType.MESH

ORDER = [
    (0, 0), (0, 1), (0, 3), (1, 0), (3, 0), (0, 2), (2, 0),
    (1, 1), (1, 3), (3, 1), (3, 3), (1, 2), (3, 2), (2, 1), (2, 3), (2, 2),
]
SLOT = {offset: i for i, offset in enumerate(ORDER)}
QUARTERS = [(0, 128), (128, 128), (256, 128), (384, 144)]
BLOCK = 528
YP, YM, ZP, ZM = (1, 0), (-1, 0), (0, 1), (0, -1)


def forward_plan():
    plan = {i: [] for i in range(16)}

    def wait(step, offset, quarters):
        plan[step].append(("wait", offset, quarters))

    def send(step, offset, quarter, direction):
        plan[step].append(("send", offset, quarter, direction))

    a, b = (0, 1), (2, 3)
    for q in a:
        send(0, (0, 0), q, ZP)
        send(0, (0, 0), q, ZM)
    for q in b:
        send(0, (0, 0), q, YP)
        send(0, (0, 0), q, YM)
    for q in a:
        send(0, (0, 0), q, YP)
        send(0, (0, 0), q, YM)
    for q in b:
        send(0, (0, 0), q, ZP)
        send(0, (0, 0), q, ZM)
    for offset in ((0, 1), (0, 3)):
        wait(1, offset, a)
    for offset in ((1, 0), (3, 0)):
        wait(1, offset, b)
    send(1, (0, 3), 0, ZP)
    send(1, (0, 1), 1, ZM)
    send(1, (3, 0), 2, YP)
    send(1, (1, 0), 3, YM)
    for q in a:
        for offset in ((0, 1), (0, 3)):
            send(1, offset, q, YP)
            send(1, offset, q, YM)
    for q in b:
        for offset in ((1, 0), (3, 0)):
            send(1, offset, q, ZP)
            send(1, offset, q, ZM)
    for offset in ((0, 1), (0, 3)):
        wait(1, offset, b)
    for offset in ((1, 0), (3, 0)):
        wait(1, offset, a)
    send(1, (0, 3), 2, ZP)
    send(1, (0, 1), 3, ZM)
    send(1, (3, 0), 0, YP)
    send(1, (1, 0), 1, YM)
    wait(5, (0, 2), a)
    wait(5, (2, 0), b)
    for q in a:
        send(5, (0, 2), q, YP)
        send(5, (0, 2), q, YM)
    for q in b:
        send(5, (2, 0), q, ZP)
        send(5, (2, 0), q, ZM)
    wait(5, (0, 2), b)
    wait(5, (2, 0), a)
    for dz in (1, 3):
        wait(7, (3, dz), a)
        wait(7, (1, dz), a)
        send(7, (3, dz), 0, YP)
        send(7, (1, dz), 1, YM)
    for dy in (1, 3):
        wait(7, (dy, 3), b)
        wait(7, (dy, 1), b)
        send(7, (dy, 3), 2, ZP)
        send(7, (dy, 1), 3, ZM)
    wait(11, (3, 2), a)
    wait(11, (1, 2), a)
    send(11, (3, 2), 0, YP)
    send(11, (1, 2), 1, YM)
    wait(11, (2, 3), b)
    wait(11, (2, 1), b)
    send(11, (2, 3), 2, ZP)
    send(11, (2, 1), 3, ZM)
    wait(11, (1, 2), b)
    wait(11, (3, 2), b)
    wait(11, (2, 1), a)
    wait(11, (2, 3), a)
    wait(15, (2, 2), a + b)
    return plan


PLAN = forward_plan()
SENDS = [e for i in range(16) for e in PLAN[i] if e[0] == "send"]


def split3(x):
    hi = x.astype(jnp.bfloat16).astype(jnp.float32)
    rest = x - hi
    mid = rest.astype(jnp.bfloat16).astype(jnp.float32)
    return hi, mid, rest - mid


def nt(a, b):
    return lax.dot_general(a, b, (((1,), (1,)), ((), ())), preferred_element_type=jnp.float32)


def tn(a, b):
    return lax.dot_general(a, b, (((0,), (0,)), ((), ())), preferred_element_type=jnp.float32)


def power_of(top):
    power = jnp.ceil(jnp.log(jnp.maximum(top, 1e-33)) * (1.0 / math.log(2.0)))
    return jnp.clip(power, -110.0, 127.0)


def quantized(x):
    top = jnp.max(jnp.abs(x), axis=0, keepdims=True)
    power = power_of(top)
    q = jnp.round(x * (jnp.exp2(15.0 - power) * 0.99)).astype(jnp.int32)
    half = x.shape[0] // 2
    words = (q[half:] << 16) | (q[:half] & 0xFFFF)
    return words, jnp.broadcast_to(power.astype(jnp.int32), (8, x.shape[1]))


def restored(words, power):
    scale = jnp.exp2(power.astype(jnp.float32) - 15.0) * (1.0 / 0.99)
    low = ((words << 16) >> 16).astype(jnp.float32) * scale
    high = (words >> 16).astype(jnp.float32) * scale
    return low, high


def attention_kernel(
    cand_hbm, scen_hbm, user_hbm, gate_hbm, norm_hbm, fwd_hbm, grad_hbm, hist_hbm, item_hbm, length_hbm,
    cand_out, rows_in, codes_in,
    cand_ref, scen_ref, user_ref, gate_ref, norm_ref, fwd_ref, grad_ref, hist_ref, item_ref, length_ref,
    buf, keys, gates, part_out, part_in, sums_out, sums_in, hist_sum, alike, matches, places_of, halves, rows_out, codes_out,
    load_sem, send_sem, recv_sem, part_send, part_recv, sums_send, sums_recv,
    rows_send, rows_recv, codes_send, codes_recv, own_sem,
):
    loads = [
        pltpu.make_async_copy(there, here, load_sem.at[i])
        for i, (there, here) in enumerate([
            (scen_hbm, scen_ref), (gate_hbm, gate_ref), (user_hbm, user_ref), (norm_hbm, norm_ref),
            (cand_hbm, cand_ref), (grad_hbm, grad_ref), (fwd_hbm, fwd_ref),
            (hist_hbm, hist_ref), (length_hbm, length_ref), (item_hbm, item_ref),
        ])
    ]
    for load in loads:
        load.start()

    dp = lax.axis_index("dp")
    seq = lax.axis_index("seq")
    x, core = dp // 2, dp % 2
    y, z = seq // 4, seq % 4

    xs = [(x + d) % 4 for d in range(4)]
    ys = [(y + d) % 4 for d in range(4)]
    zs = [(z + d) % 4 for d in range(4)]
    cores = [core, 1 - core]

    def device(dy, dz):
        return (dp, ys[dy % 4] * 4 + zs[dz % 4])

    barrier = pltpu.get_barrier_semaphore()

    lines = [(ys[d] * 4 + z, dp) for d in range(1, 4)] + [(y * 4 + zs[d], dp) for d in range(1, 4)]
    lines += [(seq, xs[d] * 2 + c) for d in range(4) for c in cores][1:]
    for there, group in lines:
        pl.semaphore_signal(barrier, inc=1, device_id=(group, there), device_id_type=MESH)

    def block_copy(number):
        _, offset, quarter, (dy, dz) = SENDS[number]
        there = SLOT[(offset[0] - dy) % 4, (offset[1] - dz) % 4]
        rows = pl.ds(*QUARTERS[quarter])
        return pltpu.make_async_remote_copy(
            src_ref=buf.at[SLOT[offset], rows],
            dst_ref=buf.at[there, rows],
            send_sem=send_sem.at[number],
            recv_sem=recv_sem.at[there, quarter],
            device_id=device(dy, dz),
            device_id_type=MESH,
        )

    def block_arrival(offset, quarter):
        rows = pl.ds(*QUARTERS[quarter])
        slot = SLOT[offset]
        return pltpu.make_async_remote_copy(
            src_ref=buf.at[slot, rows],
            dst_ref=buf.at[slot, rows],
            send_sem=send_sem.at[0],
            recv_sem=recv_sem.at[slot, quarter],
            device_id=device(0, 1),
            device_id_type=MESH,
        )

    def part_copy(i, half):
        dy, dz = ORDER[i]
        step, across = (dz, dy) if half == 0 else (dy, dz)
        there = part_in.at[half, 3 - step, across]
        return pltpu.make_async_remote_copy(
            src_ref=part_out.at[i, half],
            dst_ref=there,
            send_sem=part_send.at[i, half],
            recv_sem=part_recv.at[half, 3 - step, across],
            device_id=device(0, step) if half == 0 else device(step, 0),
            device_id_type=MESH,
        )

    parts = [(i, h) for i in range(1, 16) for h in range(2) if ORDER[i][1 - h]]

    def sums_copy(half, step):
        return pltpu.make_async_remote_copy(
            src_ref=sums_out.at[half, step - 1],
            dst_ref=sums_in.at[half, 3 - step],
            send_sem=sums_send.at[half, step - 1],
            recv_sem=sums_recv.at[half, 3 - step],
            device_id=device(step, 0) if half == 0 else device(0, step),
            device_id_type=MESH,
        )

    for load in loads[:7]:
        load.wait()
    scen_rows = scen_ref[...] == lax.broadcasted_iota(jnp.int32, (16, 256), 0)
    gates[...] = lax.dot_general(
        scen_rows.astype(jnp.float32), gate_ref[...], (((0,), (0,)), ((), ())),
        precision=lax.Precision.HIGHEST, preferred_element_type=jnp.float32,
    )
    queries = (cand_ref[...].astype(jnp.float32) * gates[...]).astype(jnp.bfloat16)
    buf[0, 0:256] = queries * jnp.bfloat16(0.0625)
    grads = grad_ref[...]
    buf[0, 256:512] = grads
    inner = lax.dot_general(
        jnp.ones((8, 256), jnp.float32),
        grads.astype(jnp.float32) * fwd_ref[...].astype(jnp.float32),
        (((1,), (1,)), ((), ())),
        precision=lax.Precision.HIGHEST, preferred_element_type=jnp.float32,
    )[0:1]
    user = (user_ref[...] - 2 * dp).astype(jnp.float32)
    numbers = [*split3(norm_ref[...]), *split3(inner), 1.0 - user, user]
    numbers = jnp.concatenate(numbers + [jnp.zeros((8, 256), jnp.float32)], axis=0)
    buf[0, 512:528] = numbers.astype(jnp.bfloat16)

    pl.semaphore_wait(barrier, 13)

    def run_plan(step):
        for event in PLAN[step]:
            if event[0] == "wait":
                for quarter in event[2]:
                    block_arrival(event[1], quarter).wait_recv()
            else:
                block_copy(SENDS.index(event)).start()

    run_plan(0)

    first = seq * 512
    places = first + lax.broadcasted_iota(jnp.int32, (512, 256), 0)
    for load in loads[7:]:
        load.wait()
    for u in range(2):
        rows = hist_ref[u].astype(jnp.float32)
        keys[u] = jnp.where(places < length_ref[u], rows, 0.0).astype(jnp.bfloat16)
    hist_sum[...] = jnp.zeros_like(hist_sum)
    def rank_items():
        items = jnp.concatenate([item_ref[0:1], item_ref[1:2]], axis=1)
        owner = items // ITEM_DEV
        other = [owner // 32, owner // 16 % 2, owner // 4 % 4, owner % 4]
        message = (other[1] + core) % 2 * 64 + (other[2] - y + 4) % 4 * 16 + (other[0] - x + 4) % 4 * 4
        message = message + (other[3] - z + 4) % 4
        found = lax.broadcasted_iota(jnp.int32, (128, 1024), 0) == message
        column = jnp.transpose(jnp.broadcast_to(items.astype(jnp.float32), (128, 1024)))[:, 0:1]
        same = column == items.astype(jnp.float32)
        one, zero = jnp.float32(1.0), jnp.float32(0.0)
        alike[...] = jnp.where(same, one, zero).astype(jnp.bfloat16)
        number = lax.broadcasted_iota(jnp.int32, (1024, 1024), 0)
        other_number = lax.broadcasted_iota(jnp.int32, (1024, 1024), 1)
        repeats = jnp.sum(jnp.where(same & (number < other_number), one, zero), axis=0, keepdims=True)
        first = jnp.where(repeats == 0.0, one, zero)
        matches[...] = jnp.where(found, first, zero)
        counts = jnp.dot(
            matches[...].astype(jnp.bfloat16), jnp.where(number <= other_number, one, zero).astype(jnp.bfloat16),
            preferred_element_type=jnp.float32,
        )
        rank = jnp.sum(matches[...] * counts, axis=0, keepdims=True) - first
        rank = jnp.dot(
            jnp.broadcast_to(rank, (8, 1024)).astype(jnp.bfloat16), alike[...], preferred_element_type=jnp.float32
        )[0:1].astype(jnp.int32)
        places_of[0:1] = message * 16 + rank
        places_of[1:2] = rank
        places_of[2:3] = (items % ITEM_DEV) * 2 + 16

    def step(k, carry):
        for i in range(1, 16):
            if PLAN[i]:
                pl.when(k == i)(lambda i=i: run_plan(i))
        numbers = buf[k, 512:528].astype(jnp.float32)
        normalizer = numbers[0:1] + numbers[1:2] + numbers[2:3]
        inner_sum = numbers[3:4] + numbers[4:5] + numbers[5:6]
        pick = [numbers[6:7], numbers[7:8]]
        low = [w.astype(jnp.bfloat16) for w in pick]
        both = buf[k, 0:512]
        query_part = jnp.zeros((256, 256), jnp.float32)
        for c in range(2):
            rows = pl.ds(c * 256, 256)
            mine = keys[0, rows] * low[0] + keys[1, rows] * low[1]
            products = nt(mine, both)
            probability = jnp.exp(products[:, :256] - normalizer)
            score_grad = (probability * (products[:, 256:] - inner_sum)).astype(jnp.bfloat16)
            weights = jnp.concatenate([score_grad, probability.astype(jnp.bfloat16)], axis=1)
            key_part = jnp.dot(weights, both, preferred_element_type=jnp.float32)
            hist_sum[0, rows] += key_part * pick[0]
            hist_sum[1, rows] += key_part * pick[1]
            query_part += tn(score_grad, mine)

        words, power = quantized(query_part)
        for h in range(2):
            columns = slice(h * 128, (h + 1) * 128)
            part_out[k, h, 0:128] = words[:, columns]
            part_out[k, h, 128:136] = power[:, columns]
        for i in range(1, 16):

            @pl.when(k == i)
            def _(i=i):
                for h in range(2):
                    if (i, h) in parts:
                        part_copy(i, h).start()

        pl.when(k == 6)(rank_items)
        return carry

    lax.fori_loop(0, 16, step, 0)

    tops = []
    for u in range(2):
        hist_sum[u] = jnp.where(places < length_ref[u], hist_sum[u], 0.0)
        top = jnp.max(jnp.abs(hist_sum[u]), axis=1, keepdims=True) * 1.01
        tops.append(jnp.broadcast_to(top, (512, 128)).astype(jnp.bfloat16))
    power = power_of(jnp.dot(alike[...], jnp.concatenate(tops, axis=0), preferred_element_type=jnp.float32))
    scale = jnp.exp2(15.0 - power) * 0.99
    for u in range(2):
        rows = pl.ds(u * 512, 512)
        for h in range(2):
            q = jnp.round(hist_sum[u, :, h * 128 : h * 128 + 128] * scale[u * 512 : u * 512 + 512]).astype(jnp.int32)
            halves[rows, h * 128 : h * 128 + 128] = (q >> 8).astype(jnp.float32).astype(jnp.bfloat16)
            halves[rows, 256 + h * 128 : 384 + h * 128] = (q & 255).astype(jnp.float32).astype(jnp.bfloat16)
    first_lane = lax.broadcasted_iota(jnp.int32, (1024, 128), 1) == 0
    power = nt(jnp.ones((8, 128), jnp.bfloat16), jnp.where(first_lane, power, 0.0).astype(jnp.bfloat16))[0:1]
    column = lax.broadcasted_iota(jnp.int32, (128, 1024), 0)
    codes = jnp.where(column < 16, places_of[2:3].astype(jnp.float32), power + 128.0)
    ranked = (column % 16 == places_of[1:2]) & (column < 32)
    codes = lax.dot_general(
        matches[...], jnp.where(ranked, codes, 0.0), (((1,), (1,)), ((), ())),
        precision=lax.Precision.HIGHEST, preferred_element_type=jnp.float32,
    )
    codes_out[...] = codes.astype(jnp.int32).reshape(128, 1, 128)

    def rows_copy(m, there):
        return pltpu.make_async_remote_copy(
            src_ref=rows_out.at[m], dst_ref=rows_in.at[m], send_sem=rows_send, recv_sem=rows_recv,
            device_id=there, device_id_type=MESH,
        )

    def codes_copy(m, there):
        return pltpu.make_async_remote_copy(
            src_ref=codes_out.at[m], dst_ref=codes_in.at[m], send_sem=codes_send, recv_sem=codes_recv,
            device_id=there, device_id_type=MESH,
        )

    own_rows = pltpu.make_async_copy(rows_out.at[0], rows_in.at[0], own_sem.at[0])
    own_codes = pltpu.make_async_copy(codes_out.at[0], codes_in.at[0], own_sem.at[1])

    def send_chunk(c, carry):
        slots = lax.broadcasted_iota(jnp.int32, (256, 1024), 0) + c * 256
        chosen = jnp.where(slots == places_of[0:1], 1.0, 0.0).astype(jnp.bfloat16)
        moved = jnp.dot(chosen, halves[...], preferred_element_type=jnp.float32).astype(jnp.int32)
        value = (moved[:, 0:256] << 8) + moved[:, 256:512]
        words = (value[:, 128:256] << 16) | (value[:, 0:128] & 0xFFFF)
        rows_out[pl.ds(c * 16, 16)] = words.reshape(16, 16, 128)

        to_core = (core + c // 4) % 2
        to_y = (y + c % 4) % 4
        for j in range(16):
            m = c * 16 + j
            there = (xs[j // 4] * 2 + to_core, to_y * 4 + zs[j % 4])

            def send_one(m=m, there=there):
                rows_copy(m, there).start()
                codes_copy(m, there).start()

            if j == 0:
                pl.when(c > 0)(send_one)
            else:
                send_one()
        return carry

    lax.fori_loop(0, 8, send_chunk, 0)
    own_rows.start()
    own_codes.start()

    for i, h in parts:
        part_copy(i, h).wait_recv()
    firsts = []
    for h in range(2):
        for d in range(4):
            own = SLOT[(d, 0) if h == 0 else (0, d)]
            low, high = restored(part_out[own, h, 0:128], part_out[own, h, 128:129])
            for source in range(3):
                a, b = restored(part_in[h, source, d, 0:128], part_in[h, source, d, 128:129])
                low, high = low + a, high + b
            if d == 0:
                firsts.append((low, high))
            else:
                words, power = quantized(jnp.concatenate([low, high], axis=0))
                sums_out[h, d - 1, 0:128] = words
                sums_out[h, d - 1, 128:136] = power
                sums_copy(h, d).start()
    for h in range(2):
        low, high = firsts[h]
        for d in range(1, 4):
            sums_copy(h, d).wait_recv()
        for source in range(3):
            a, b = restored(sums_in[h, source, 0:128], sums_in[h, source, 128:129])
            low, high = low + a, high + b
        columns = slice(h * 128, (h + 1) * 128)
        cand_out[0:128, columns] = low * 0.0625 * gates[0:128, columns]
        cand_out[128:256, columns] = high * 0.0625 * gates[128:256, columns]
    for number in range(len(SENDS)):
        block_copy(number).wait_send()
    for i, h in parts:
        part_copy(i, h).wait_send()
    for h in range(2):
        for d in range(1, 4):
            sums_copy(h, d).wait_send()
    own_rows.wait()
    own_codes.wait()
    others = pl.ds(1, 127)
    all_rows = pltpu.make_async_remote_copy(
        src_ref=rows_out.at[others], dst_ref=rows_in.at[others], send_sem=rows_send, recv_sem=rows_recv,
        device_id=device(0, 1), device_id_type=MESH,
    )
    all_codes = pltpu.make_async_remote_copy(
        src_ref=codes_out.at[others], dst_ref=codes_in.at[others], send_sem=codes_send, recv_sem=codes_recv,
        device_id=device(0, 1), device_id_type=MESH,
    )
    all_rows.wait()
    all_codes.wait()


def table_kernel(
    rows_hbm, codes_hbm, cand_hbm, table_out, cand_out,
    rows_ref, codes_ref, powers_ref, cand_ref, values, t0, t1, table, sem
):
    loads = [
        pltpu.make_async_copy(codes_hbm, codes_ref, sem.at[9]),
        pltpu.make_async_copy(codes_hbm, powers_ref, sem.at[10]),
        pltpu.make_async_copy(rows_hbm, rows_ref, sem.at[11]),
        pltpu.make_async_copy(cand_hbm, cand_ref, sem.at[12]),
    ]
    for load in loads:
        load.start()
    cand_copy = pltpu.make_async_copy(cand_ref, cand_out, sem.at[8])

    def clear(c, carry):
        for t in (t0, t1):
            t[pl.ds(c * 1024, 1024)] = jnp.zeros((1024, 128), jnp.float32)
        return carry

    lax.fori_loop(0, 8, clear, 0)
    for t in (t0, t1):
        t[8192:8208] = jnp.zeros((16, 128), jnp.float32)

    for load in loads:
        load.wait()
    cand_copy.start()
    powers = jnp.transpose(powers_ref[...].astype(jnp.float32))[16:32]
    scales = jnp.exp2(powers - 143.0) * (1.0 / 0.99)
    for m in range(128):
        scale = scales[:, m : m + 1]
        words = rows_ref[m * 16 : m * 16 + 16]
        values[pl.ds(m * 32, 16, stride=2)] = ((words << 16) >> 16).astype(jnp.float32) * scale
        values[pl.ds(m * 32 + 1, 16, stride=2)] = (words >> 16).astype(jnp.float32) * scale

    def add_messages(i, carry):
        for t, m in ((t0, i * 2), (t1, i * 2 + 1)):
            places = [pl.ds(pl.multiple_of(codes_ref[m, j], 2), 2) for j in range(16)]
            sums = [t[places[j]] + values[pl.ds(m * 32 + j * 2, 2)] for j in range(16)]
            for j in range(16):
                t[places[j]] = sums[j]
        return carry

    lax.fori_loop(0, 64, add_messages, 0)

    def out_copy(c):
        rows = pl.ds(c * 512, 512)
        return pltpu.make_async_copy(table.at[rows], table_out.at[rows], sem.at[c])

    for c in range(8):
        for h in range(2):
            rows = pl.ds(16 + c * 1024 + h, 512, stride=2)
            table[c * 512 : c * 512 + 512, h * 128 : h * 128 + 128] = t0[rows] + t1[rows]
        out_copy(c).start()
    for c in range(8):
        out_copy(c).wait()
    cand_copy.wait()


def add_rows(rows, codes, candidate_grad):
    hbm = pl.BlockSpec(memory_space=pltpu.HBM)
    return pl.pallas_call(
        table_kernel,
        out_shape=(
            jax.ShapeDtypeStruct((ITEM_DEV, 256), jnp.float32),
            jax.ShapeDtypeStruct((256, 256), jnp.float32),
        ),
        in_specs=[hbm, hbm, hbm],
        out_specs=(hbm, hbm),
        scratch_shapes=[
            pltpu.VMEM((2048, 128), jnp.int32),
            pltpu.SMEM((128, 128), jnp.int32),
            pltpu.VMEM((128, 128), jnp.int32),
            pltpu.VMEM((256, 256), jnp.float32),
            pltpu.VMEM((4096, 128), jnp.float32),
            pltpu.VMEM((2 * ITEM_DEV + 16, 128), jnp.float32),
            pltpu.VMEM((2 * ITEM_DEV + 16, 128), jnp.float32),
            pltpu.VMEM((ITEM_DEV, 256), jnp.float32),
            pltpu.SemaphoreType.DMA((13,)),
        ],
        compiler_params=pltpu.CompilerParams(vmem_limit_bytes=64 * 1024 * 1024),
        cost_estimate=pl.CostEstimate(flops=2_000_000, bytes_accessed=5_500_000, transcendentals=0),
        name="table_rows",
    )(rows, codes, candidate_grad)


def attention(candidates, scenarios, users, gate_table, normalizer, forward_out, out_grad, history, items, lengths):
    vmem = pl.BlockSpec(memory_space=pltpu.VMEM)
    return pl.pallas_call(
        attention_kernel,
        out_shape=(
            jax.ShapeDtypeStruct((256, 256), jnp.float32),
            jax.ShapeDtypeStruct((128, 16, 128), jnp.int32),
            jax.ShapeDtypeStruct((128, 1, 128), jnp.int32),
        ),
        in_specs=[pl.BlockSpec(memory_space=pltpu.HBM)] * 10,
        out_specs=(vmem, pl.BlockSpec(memory_space=pl.ANY), pl.BlockSpec(memory_space=pl.ANY)),
        scratch_shapes=[
            pltpu.VMEM((256, 256), jnp.bfloat16),
            pltpu.VMEM((1, 256), jnp.int32),
            pltpu.VMEM((1, 256), jnp.int32),
            pltpu.VMEM((16, 256), jnp.float32),
            pltpu.VMEM((1, 256), jnp.float32),
            pltpu.VMEM((256, 256), jnp.bfloat16),
            pltpu.VMEM((256, 256), jnp.bfloat16),
            pltpu.VMEM((2, 512, 256), jnp.bfloat16),
            pltpu.VMEM((2, 512), jnp.int32),
            pltpu.SMEM((2,), jnp.int32),
            pltpu.VMEM((16, BLOCK, 256), jnp.bfloat16),
            pltpu.VMEM((2, 512, 256), jnp.bfloat16),
            pltpu.VMEM((256, 256), jnp.float32),
            pltpu.VMEM((16, 2, 136, 128), jnp.int32),
            pltpu.VMEM((2, 3, 4, 136, 128), jnp.int32),
            pltpu.VMEM((2, 3, 136, 128), jnp.int32),
            pltpu.VMEM((2, 3, 136, 128), jnp.int32),
            pltpu.VMEM((2, 512, 256), jnp.float32),
            pltpu.VMEM((1024, 1024), jnp.bfloat16),
            pltpu.VMEM((128, 1024), jnp.float32),
            pltpu.VMEM((8, 1024), jnp.int32),
            pltpu.VMEM((1024, 512), jnp.bfloat16),
            pltpu.VMEM((128, 16, 128), jnp.int32),
            pltpu.VMEM((128, 1, 128), jnp.int32),
            pltpu.SemaphoreType.DMA((10,)),
            pltpu.SemaphoreType.DMA((len(SENDS),)),
            pltpu.SemaphoreType.DMA((16, 4)),
            pltpu.SemaphoreType.DMA((16, 2)),
            pltpu.SemaphoreType.DMA((2, 3, 4)),
            pltpu.SemaphoreType.DMA((2, 3)),
            pltpu.SemaphoreType.DMA((2, 3)),
            pltpu.SemaphoreType.DMA,
            pltpu.SemaphoreType.DMA,
            pltpu.SemaphoreType.DMA,
            pltpu.SemaphoreType.DMA,
            pltpu.SemaphoreType.DMA((2,)),
        ],
        compiler_params=pltpu.CompilerParams(
            collective_id=0, has_side_effects=True, vmem_limit_bytes=64 * 1024 * 1024
        ),
        cost_estimate=pl.CostEstimate(
            flops=5_400_000_000, bytes_accessed=4_000_000, transcendentals=2_100_000
        ),
        name="attention_grads",
    )(
        candidates, scenarios.reshape(1, -1), users.reshape(1, -1), gate_table, normalizer.reshape(1, -1),
        forward_out, out_grad, history, items, lengths,
    )


def local(
    candidates,
    scenarios,
    candidate_user,
    gate_table,
    log_normalizer,
    forward_out,
    out_grad,
    history,
    history_length,
    history_items,
):
    candidate_grad, rows, codes = attention(
        candidates, scenarios, candidate_user, gate_table, log_normalizer,
        forward_out, out_grad, history, history_items, history_length,
    )
    table_grad, candidate_grad = add_rows(rows.reshape(2048, 128), codes.reshape(128, 128), candidate_grad)
    return (candidate_grad, table_grad)


def solution(mesh):
    return jax.shard_map(
        local,
        mesh=mesh,
        in_specs=(
            P(("dp", "seq"), None),
            P(("dp", "seq")),
            P(("dp", "seq")),
            P(),
            P(("dp", "seq")),
            P(("dp", "seq"), None),
            P(("dp", "seq"), None),
            P("dp", "seq", None),
            P("dp"),
            P("dp", "seq"),
        ),
        out_specs=(P(("dp", "seq"), None), P(("dp", "seq"), None)),
        check_vma=False,
    )
```

profile of v0, /device:TPU:0, one launch (start us, length us, event | category | flops | bytes accessed | tf_op | source)
XLA Modules:
  0.0 70.4 jit_solution(13392168889359669594)
XLA Ops:
  0.6 62.4 %attention_grads.1 = (f32[256,256]{1,0:T(8,128)}, s32[128,16,128]{2,1,0:T(8,128)}, s32[128,1,128]{2,1,0:T(1,128)}) custom-call(bf16[256,256]{1,0:T(8,128)(2,1)} %cand_hbm.1, s32[1,256]{1,0:T(1,128)} %bitcast.7, s32[1,256]{1,0:T(1,128)} %bitcast.8, f32[16,256]{1,0:T(8,128)} %gate_hbm.1, f32[1,256]{1,0:T(1,128)} %bitcast.9, bf16[256,256]{1,0:T(8,128)(2,1)} %fwd_hbm.1, ...), custom_call_target="tpu_custom_call" | custom-call | flops 5400000000 | bytes 4000000 | tf_op jit(solution)/shard_map/attention_grads/pallas_call | solution.py:548
  63.1 7.3 %table_rows.1 = (f32[4096,256]{1,0:T(8,128)}, f32[256,256]{1,0:T(8,128)}) custom-call(s32[2048,128]{1,0:T(8,128)} %bitcast.5, s32[128,128]{1,0:T(8,128)} %bitcast.6, f32[256,256]{1,0:T(8,128)} %get-tuple-element.9.cand_hbm), custom_call_target="tpu_custom_call" | custom-call | flops 2000000 | bytes 5500000 | tf_op jit(solution)/shard_map/table_rows/pallas_call | solution.py:521
where the time goes:
time: 71 us; the launch traced here: 70.4 us
  Pallas kernels  69.8 us (98%)
    pallas_call x1, Pallas kernels, attention(): pl.pallas_call(attention_kernel, out_shape=(jax.ShapeDtypeStruct((256, 25...  62.4 us
    pallas_call x1, Pallas kernels, add_rows(): pl.pallas_call(table_kernel, out_shape=(jax.ShapeDtypeStruct((ITEM_DEV, 2...  7.34 us

commit v1 on v0

--- a/solution.py
+++ b/solution.py
@@ -11,8 +11,8 @@
 MESH = pl.DeviceIdType.MESH
 
 ORDER = [
-    (0, 0), (0, 1), (0, 3), (1, 0), (3, 0), (0, 2), (2, 0),
-    (1, 1), (1, 3), (3, 1), (3, 3), (1, 2), (3, 2), (2, 1), (2, 3), (2, 2),
+    (0, 0), (0, 1), (0, 3), (1, 0), (3, 0), (1, 1), (1, 3), (3, 1), (3, 3),
+    (0, 2), (2, 0), (1, 2), (2, 1), (3, 2), (2, 3), (2, 2),
 ]
 SLOT = {offset: i for i, offset in enumerate(ORDER)}
 QUARTERS = [(0, 128), (128, 128), (256, 128), (384, 144)]
@@ -42,62 +42,68 @@
     for q in b:
         send(0, (0, 0), q, ZP)
         send(0, (0, 0), q, ZM)
-    for offset in ((0, 1), (0, 3)):
-        wait(1, offset, a)
-    for offset in ((1, 0), (3, 0)):
-        wait(1, offset, b)
-    send(1, (0, 3), 0, ZP)
-    send(1, (0, 1), 1, ZM)
-    send(1, (3, 0), 2, YP)
-    send(1, (1, 0), 3, YM)
-    for q in a:
+    for q in (0, 1):
         for offset in ((0, 1), (0, 3)):
-            send(1, offset, q, YP)
-            send(1, offset, q, YM)
-    for q in b:
+            wait(1, offset, (a[q],))
         for offset in ((1, 0), (3, 0)):
-            send(1, offset, q, ZP)
-            send(1, offset, q, ZM)
-    for offset in ((0, 1), (0, 3)):
-        wait(1, offset, b)
-    for offset in ((1, 0), (3, 0)):
-        wait(1, offset, a)
-    send(1, (0, 3), 2, ZP)
-    send(1, (0, 1), 3, ZM)
-    send(1, (3, 0), 0, YP)
-    send(1, (1, 0), 1, YM)
-    wait(5, (0, 2), a)
-    wait(5, (2, 0), b)
-    for q in a:
-        send(5, (0, 2), q, YP)
-        send(5, (0, 2), q, YM)
-    for q in b:
-        send(5, (2, 0), q, ZP)
-        send(5, (2, 0), q, ZM)
-    wait(5, (0, 2), b)
-    wait(5, (2, 0), a)
-    for dz in (1, 3):
-        wait(7, (3, dz), a)
-        wait(7, (1, dz), a)
-        send(7, (3, dz), 0, YP)
-        send(7, (1, dz), 1, YM)
-    for dy in (1, 3):
-        wait(7, (dy, 3), b)
-        wait(7, (dy, 1), b)
-        send(7, (dy, 3), 2, ZP)
-        send(7, (dy, 1), 3, ZM)
-    wait(11, (3, 2), a)
-    wait(11, (1, 2), a)
-    send(11, (3, 2), 0, YP)
-    send(11, (1, 2), 1, YM)
-    wait(11, (2, 3), b)
-    wait(11, (2, 1), b)
-    send(11, (2, 3), 2, ZP)
-    send(11, (2, 1), 3, ZM)
+            wait(1, offset, (b[q],))
+        if q == 0:
+            send(1, (0, 3), 0, ZP)
+            send(1, (3, 0), 2, YP)
+        else:
+            send(1, (0, 1), 1, ZM)
+            send(1, (1, 0), 3, YM)
+        for offset in ((0, 1), (0, 3)):
+            send(1, offset, a[q], YP)
+            send(1, offset, a[q], YM)
+        for offset in ((1, 0), (3, 0)):
+            send(1, offset, b[q], ZP)
+            send(1, offset, b[q], ZM)
+    for q in (0, 1):
+        for offset in ((0, 1), (0, 3)):
+            wait(1, offset, (b[q],))
+        for offset in ((1, 0), (3, 0)):
+            wait(1, offset, (a[q],))
+        if q == 0:
+            send(1, (0, 3), 2, ZP)
+            send(1, (3, 0), 0, YP)
+        else:
+            send(1, (0, 1), 3, ZM)
+            send(1, (1, 0), 1, YM)
+    for q in (0, 1):
+        wait(3, (0, 2), (a[q],))
+        wait(3, (2, 0), (b[q],))
+        send(3, (0, 2), a[q], YP)
+        send(3, (0, 2), a[q], YM)
+        send(3, (2, 0), b[q], ZP)
+        send(3, (2, 0), b[q], ZM)
+    wait(5, (1, 1), a + b)
+    send(5, (1, 1), 1, YM)
+    send(5, (1, 1), 3, ZM)
+    wait(6, (1, 3), a + b)
+    send(6, (1, 3), 1, YM)
+    send(6, (1, 3), 2, ZP)
+    wait(6, (3, 1), a + b)
+    send(6, (3, 1), 0, YP)
+    send(6, (3, 1), 3, ZM)
+    wait(6, (3, 3), a + b)
+    send(6, (3, 3), 0, YP)
+    send(6, (3, 3), 2, ZP)
+    wait(9, (0, 2), b)
+    wait(9, (2, 0), a)
+    wait(10, (3, 2), a)
+    wait(10, (1, 2), a)
+    send(10, (3, 2), 0, YP)
+    send(10, (1, 2), 1, YM)
+    wait(10, (2, 3), b)
+    wait(10, (2, 1), b)
+    send(10, (2, 3), 2, ZP)
+    send(10, (2, 1), 3, ZM)
+    plan[11] += [("parts", i) for i in range(1, 11)]
     wait(11, (1, 2), b)
-    wait(11, (3, 2), b)
-    wait(11, (2, 1), a)
-    wait(11, (2, 3), a)
+    wait(12, (2, 1), a)
+    wait(13, (3, 2), b)
+    wait(14, (2, 3), a)
     wait(15, (2, 2), a + b)
     return plan
 
@@ -144,17 +150,17 @@
 
 def attention_kernel(
     cand_hbm, scen_hbm, user_hbm, gate_hbm, norm_hbm, fwd_hbm, grad_hbm, hist_hbm, item_hbm, length_hbm,
-    cand_out, rows_in, codes_in,
-    cand_ref, scen_ref, user_ref, gate_ref, norm_ref, fwd_ref, grad_ref, hist_ref, item_ref, length_ref,
-    buf, keys, gates, part_out, part_in, sums_out, sums_in, hist_sum, alike, matches, places_of, halves, rows_out, codes_out,
-    load_sem, send_sem, recv_sem, part_send, part_recv, sums_send, sums_recv,
+    cand_out, rows_in, codes_out_t,
+    cand_ref, scen_ref, user_ref, gate_ref, norm_ref, fwd_ref, hist_ref, item_ref, length_ref,
+    buf, keys, gates, part_out, part_in, mid_out, mid_in, sums_out, sums_in, hist_sum, alike, matches, places_of, halves, rows_out, codes_out, codes_in, code_rows, code_spots,
+    load_sem, send_sem, recv_sem, part_send, part_recv, mid_send, mid_recv, sums_send, sums_recv,
     rows_send, rows_recv, codes_send, codes_recv, own_sem,
 ):
     loads = [
         pltpu.make_async_copy(there, here, load_sem.at[i])
         for i, (there, here) in enumerate([
-            (scen_hbm, scen_ref), (gate_hbm, gate_ref), (user_hbm, user_ref), (norm_hbm, norm_ref),
-            (cand_hbm, cand_ref), (grad_hbm, grad_ref), (fwd_hbm, fwd_ref),
+            (grad_hbm, buf.at[0, pl.ds(256, 256)]), (scen_hbm, scen_ref), (gate_hbm, gate_ref),
+            (cand_hbm, cand_ref), (user_hbm, user_ref), (norm_hbm, norm_ref), (fwd_hbm, fwd_ref),
             (hist_hbm, hist_ref), (length_hbm, length_ref), (item_hbm, item_ref),
         ])
     ]
@@ -206,20 +212,59 @@
             device_id_type=MESH,
         )
 
-    def part_copy(i, half):
-        dy, dz = ORDER[i]
-        step, across = (dz, dy) if half == 0 else (dy, dz)
-        there = part_in.at[half, 3 - step, across]
+    def line_copy(source, there, half, step, send, recv):
         return pltpu.make_async_remote_copy(
-            src_ref=part_out.at[i, half],
-            dst_ref=there,
-            send_sem=part_send.at[i, half],
-            recv_sem=part_recv.at[half, 3 - step, across],
+            src_ref=source, dst_ref=there, send_sem=send, recv_sem=recv,
             device_id=device(0, step) if half == 0 else device(step, 0),
             device_id_type=MESH,
         )
 
-    parts = [(i, h) for i in range(1, 16) for h in range(2) if ORDER[i][1 - h]]
+    def route(i, half):
+        dy, dz = ORDER[i]
+        return (dz, dy) if half == 0 else (dy, dz)
+
+    def toward(across):
+        return -1 if across % 2 == 0 else 1
+
+    def part_copy(i, half):
+        step, across = route(i, half)
+        send = part_send.at[i, half]
+        if step == 2:
+            there, recv, step = mid_in.at[half, across], mid_recv.at[half, across], toward(across)
+        else:
+            there, recv, step = part_in.at[half, 1, across], part_recv.at[half, 1, across], -toward(across)
+        return line_copy(part_out.at[i, half], there, half, step, send, recv)
+
+    def mid_copy(half, across):
+        return line_copy(
+            mid_out.at[half, across], part_in.at[half, 0, across], half, toward(across),
+            mid_send.at[half, across], part_recv.at[half, 0, across],
+        )
+
+    parts = []
+    for i in range(1, 16):
+        for h in range(2):
+            step, across = route(i, h)
+            if step == 2 or (step and step % 4 == -toward(across) % 4):
+                parts.append((i, h))
+
+    def send_parts(i):
+        for h in range(2):
+            if (i, h) in parts:
+                part_copy(i, h).start()
+
+    def pass_on(h, across):
+        step = toward(across) % 4
+        own = SLOT[(across, step) if h == 0 else (step, across)]
+        line_copy(
+            mid_out.at[h, across], mid_in.at[h, across], h, 1, mid_send.at[h, across], mid_recv.at[h, across]
+        ).wait_recv()
+        low, high = restored(part_out[own, h, 0:128], part_out[own, h, 128:129])
+        a, b = restored(mid_in[h, across, 0:128], mid_in[h, across, 128:129])
+        words, power = quantized(jnp.concatenate([low + a, high + b], axis=0))
+        mid_out[h, across, 0:128] = words
+        mid_out[h, across, 128:136] = power
+        mid_copy(h, across).start()
 
     def sums_copy(half, step):
         return pltpu.make_async_remote_copy(
@@ -231,7 +276,23 @@
             device_id_type=MESH,
         )
 
-    for load in loads[:7]:
+    def run_plan(step):
+        for event in PLAN[step]:
+            if event[0] == "wait":
+                for quarter in event[2]:
+                    block_arrival(event[1], quarter).wait_recv()
+            elif event[0] == "send":
+                block_copy(SENDS.index(event)).start()
+            else:
+                send_parts(event[1])
+
+    early = [event for event in PLAN[0] if event[2] == 2]
+    late = [event for event in PLAN[0] if event[2] != 2]
+    loads[0].wait()
+    pl.semaphore_wait(barrier, 13)
+    for event in early:
+        block_copy(SENDS.index(event)).start()
+    for load in loads[1:7]:
         load.wait()
     scen_rows = scen_ref[...] == lax.broadcasted_iota(jnp.int32, (16, 256), 0)
     gates[...] = lax.dot_general(
@@ -240,8 +301,7 @@
     )
     queries = (cand_ref[...].astype(jnp.float32) * gates[...]).astype(jnp.bfloat16)
     buf[0, 0:256] = queries * jnp.bfloat16(0.0625)
-    grads = grad_ref[...]
-    buf[0, 256:512] = grads
+    grads = buf[0, 256:512]
     inner = lax.dot_general(
         jnp.ones((8, 256), jnp.float32),
         grads.astype(jnp.float32) * fwd_ref[...].astype(jnp.float32),
@@ -253,17 +313,8 @@
     numbers = jnp.concatenate(numbers + [jnp.zeros((8, 256), jnp.float32)], axis=0)
     buf[0, 512:528] = numbers.astype(jnp.bfloat16)
 
-    pl.semaphore_wait(barrier, 13)
-
-    def run_plan(step):
-        for event in PLAN[step]:
-            if event[0] == "wait":
-                for quarter in event[2]:
-                    block_arrival(event[1], quarter).wait_recv()
-            else:
-                block_copy(SENDS.index(event)).start()
-
-    run_plan(0)
+    for event in late:
+        block_copy(SENDS.index(event)).start()
 
     first = seq * 512
     places = first + lax.broadcasted_iota(jnp.int32, (512, 256), 0)
@@ -277,8 +328,8 @@
         items = jnp.concatenate([item_ref[0:1], item_ref[1:2]], axis=1)
         owner = items // ITEM_DEV
         other = [owner // 32, owner // 16 % 2, owner // 4 % 4, owner % 4]
-        message = (other[1] + core) % 2 * 64 + (other[2] - y + 4) % 4 * 16 + (other[0] - x + 4) % 4 * 4
-        message = message + (other[3] - z + 4) % 4
+        off_x, off_y, off_z = (other[0] - x + 4) % 4, (other[2] - y + 4) % 4, (other[3] - z + 4) % 4
+        message = (other[1] + core) % 2 * 64 + (off_z + 8 - off_x - off_y) % 4 * 16 + off_y * 4 + off_x
         found = lax.broadcasted_iota(jnp.int32, (128, 1024), 0) == message
         column = jnp.transpose(jnp.broadcast_to(items.astype(jnp.float32), (128, 1024)))[:, 0:1]
         same = column == items.astype(jnp.float32)
@@ -299,48 +350,72 @@
         )[0:1].astype(jnp.int32)
         places_of[0:1] = message * 16 + rank
         places_of[1:2] = rank
-        places_of[2:3] = (items % ITEM_DEV) * 2 + 16
-
-    def step(k, carry):
-        for i in range(1, 16):
-            if PLAN[i]:
-                pl.when(k == i)(lambda i=i: run_plan(i))
+        place = (items % ITEM_DEV) * 2 + 16
+        column = lax.broadcasted_iota(jnp.int32, (128, 1024), 0)
+        number = jnp.where(column < 16, place % 256, jnp.where(column < 32, 0, place // 256))
+        ranked = (column % 16 == rank) & (column < 48)
+        code_rows[...] = jnp.where(ranked, number, 0).astype(jnp.float32)
+        code_spots[...] = jnp.where(ranked & (column >= 16) & (column < 32), one, zero)
+
+    def products_of(k):
         numbers = buf[k, 512:528].astype(jnp.float32)
         normalizer = numbers[0:1] + numbers[1:2] + numbers[2:3]
         inner_sum = numbers[3:4] + numbers[4:5] + numbers[5:6]
         pick = [numbers[6:7], numbers[7:8]]
         low = [w.astype(jnp.bfloat16) for w in pick]
         both = buf[k, 0:512]
-        query_part = jnp.zeros((256, 256), jnp.float32)
-        for c in range(2):
-            rows = pl.ds(c * 256, 256)
-            mine = keys[0, rows] * low[0] + keys[1, rows] * low[1]
-            products = nt(mine, both)
-            probability = jnp.exp(products[:, :256] - normalizer)
-            score_grad = (probability * (products[:, 256:] - inner_sum)).astype(jnp.bfloat16)
-            weights = jnp.concatenate([score_grad, probability.astype(jnp.bfloat16)], axis=1)
-            key_part = jnp.dot(weights, both, preferred_element_type=jnp.float32)
-            hist_sum[0, rows] += key_part * pick[0]
-            hist_sum[1, rows] += key_part * pick[1]
-            query_part += tn(score_grad, mine)
-
+        mine = keys[0] * low[0] + keys[1] * low[1]
+        products = nt(mine, both)
+        probability = jnp.exp(products[:, :256] - normalizer)
+        score_grad = (probability * (products[:, 256:] - inner_sum)).astype(jnp.bfloat16)
+        weights = jnp.concatenate([score_grad, probability.astype(jnp.bfloat16)], axis=1)
+        key_part = jnp.dot(weights, both, preferred_element_type=jnp.float32)
+        return pick, key_part, tn(score_grad, mine)
+
+    def keep_part(k, query_part):
         words, power = quantized(query_part)
         for h in range(2):
             columns = slice(h * 128, (h + 1) * 128)
             part_out[k, h, 0:128] = words[:, columns]
             part_out[k, h, 128:136] = power[:, columns]
-        for i in range(1, 16):
+
+    def one_step(k):
+        pick, key_part, query_part = products_of(k)
+        hist_sum[0] += key_part * pick[0]
+        hist_sum[1] += key_part * pick[1]
+        keep_part(k, query_part)
+
+    def two_steps(n, carry):
+        k = n * 2 + 1
+        for i in range(1, 15, 2):
+            if PLAN[i] or PLAN[i + 1]:
+
+                @pl.when(k == i)
+                def _(i=i):
+                    run_plan(i)
+                    run_plan(i + 1)
+
+        pick, key_part, query_part = products_of(k)
+        next_pick, next_key_part, next_query_part = products_of(k + 1)
+        for u in range(2):
+            hist_sum[u] += key_part * pick[u] + next_key_part * next_pick[u]
+        keep_part(k, query_part)
+        keep_part(k + 1, next_query_part)
+        for i in range(11, 15, 2):
 
             @pl.when(k == i)
             def _(i=i):
-                for h in range(2):
-                    if (i, h) in parts:
-                        part_copy(i, h).start()
-
-        pl.when(k == 6)(rank_items)
+                send_parts(i)
+                send_parts(i + 1)
+
         return carry
 
-    lax.fori_loop(0, 16, step, 0)
+    one_step(0)
+    rank_items()
+    lax.fori_loop(0, 7, two_steps, 0)
+    run_plan(15)
+    one_step(15)
+    send_parts(15)
 
     tops = []
     for u in range(2):
@@ -357,12 +432,9 @@
             halves[rows, 256 + h * 128 : 384 + h * 128] = (q & 255).astype(jnp.float32).astype(jnp.bfloat16)
     first_lane = lax.broadcasted_iota(jnp.int32, (1024, 128), 1) == 0
     power = nt(jnp.ones((8, 128), jnp.bfloat16), jnp.where(first_lane, power, 0.0).astype(jnp.bfloat16))[0:1]
-    column = lax.broadcasted_iota(jnp.int32, (128, 1024), 0)
-    codes = jnp.where(column < 16, places_of[2:3].astype(jnp.float32), power + 128.0)
-    ranked = (column % 16 == places_of[1:2]) & (column < 32)
-    codes = lax.dot_general(
-        matches[...], jnp.where(ranked, codes, 0.0), (((1,), (1,)), ((), ())),
-        precision=lax.Precision.HIGHEST, preferred_element_type=jnp.float32,
+    codes = nt(
+        matches[...].astype(jnp.bfloat16),
+        (code_rows[...] + code_spots[...] * (power + 128.0)).astype(jnp.bfloat16),
     )
     codes_out[...] = codes.astype(jnp.int32).reshape(128, 1, 128)
 
@@ -390,10 +462,10 @@
         rows_out[pl.ds(c * 16, 16)] = words.reshape(16, 16, 128)
 
         to_core = (core + c // 4) % 2
-        to_y = (y + c % 4) % 4
+        to_z = [(z + c + d) % 4 for d in range(4)]
         for j in range(16):
             m = c * 16 + j
-            there = (xs[j // 4] * 2 + to_core, to_y * 4 + zs[j % 4])
+            there = (xs[j % 4] * 2 + to_core, ys[j // 4] * 4 + to_z[(j + j // 4) % 4])
 
             def send_one(m=m, there=there):
                 rows_copy(m, there).start()
@@ -405,18 +477,27 @@
                 send_one()
         return carry
 
+    for across in (0, 1, 3, 2):
+        for h in range(2):
+            pass_on(h, across)
+
     lax.fori_loop(0, 8, send_chunk, 0)
     own_rows.start()
     own_codes.start()
 
-    for i, h in parts:
-        part_copy(i, h).wait_recv()
+    for h in range(2):
+        for j in range(2):
+            for across in range(4):
+                line_copy(
+                    part_in.at[h, j, across], part_in.at[h, j, across], h, 1,
+                    mid_send.at[h, across], part_recv.at[h, j, across],
+                ).wait_recv()
     firsts = []
     for h in range(2):
         for d in range(4):
             own = SLOT[(d, 0) if h == 0 else (0, d)]
             low, high = restored(part_out[own, h, 0:128], part_out[own, h, 128:129])
-            for source in range(3):
+            for source in range(2):
                 a, b = restored(part_in[h, source, d, 0:128], part_in[h, source, d, 128:129])
                 low, high = low + a, high + b
             if d == 0:
@@ -441,6 +522,9 @@
     for i, h in parts:
         part_copy(i, h).wait_send()
     for h in range(2):
+        for across in range(4):
+            mid_copy(h, across).wait_send()
+    for h in range(2):
         for d in range(1, 4):
             sums_copy(h, d).wait_send()
     own_rows.wait()
@@ -454,8 +538,11 @@
         src_ref=codes_out.at[others], dst_ref=codes_in.at[others], send_sem=codes_send, recv_sem=codes_recv,
         device_id=device(0, 1), device_id_type=MESH,
     )
+    all_codes.wait()
+    got = jnp.transpose(codes_in[...].reshape(128, 128).astype(jnp.float32)).astype(jnp.int32)
+    codes_out_t[0:16] = got[0:16] + got[32:48] * 256
+    codes_out_t[16:32] = got[16:32]
     all_rows.wait()
-    all_codes.wait()
 
 
 def table_kernel(
@@ -463,11 +550,13 @@
     rows_ref, codes_ref, powers_ref, cand_ref, values, t0, t1, table, sem
 ):
     loads = [
-        pltpu.make_async_copy(codes_hbm, codes_ref, sem.at[9]),
-        pltpu.make_async_copy(codes_hbm, powers_ref, sem.at[10]),
-        pltpu.make_async_copy(rows_hbm, rows_ref, sem.at[11]),
-        pltpu.make_async_copy(cand_hbm, cand_ref, sem.at[12]),
+        pltpu.make_async_copy(codes_hbm.at[0:16], codes_ref, sem.at[9]),
+        pltpu.make_async_copy(codes_hbm.at[16:32], powers_ref, sem.at[10]),
+        pltpu.make_async_copy(cand_hbm, cand_ref, sem.at[11]),
     ]
+    for part in range(4):
+        rows = pl.ds(part * 512, 512)
+        loads.append(pltpu.make_async_copy(rows_hbm.at[rows], rows_ref.at[rows], sem.at[12 + part]))
     for load in loads:
         load.start()
     cand_copy = pltpu.make_async_copy(cand_ref, cand_out, sem.at[8])
@@ -481,23 +570,27 @@
     for t in (t0, t1):
         t[8192:8208] = jnp.zeros((16, 128), jnp.float32)
 
-    for load in loads:
+    for load in loads[:3]:
         load.wait()
     cand_copy.start()
-    powers = jnp.transpose(powers_ref[...].astype(jnp.float32))[16:32]
-    scales = jnp.exp2(powers - 143.0) * (1.0 / 0.99)
+    scales = jnp.exp2(powers_ref[...].astype(jnp.float32) - 143.0) * (1.0 / 0.99)
     for m in range(128):
+        if m % 32 == 0:
+            loads[3 + m // 32].wait()
         scale = scales[:, m : m + 1]
         words = rows_ref[m * 16 : m * 16 + 16]
         values[pl.ds(m * 32, 16, stride=2)] = ((words << 16) >> 16).astype(jnp.float32) * scale
         values[pl.ds(m * 32 + 1, 16, stride=2)] = (words >> 16).astype(jnp.float32) * scale
 
     def add_messages(i, carry):
-        for t, m in ((t0, i * 2), (t1, i * 2 + 1)):
-            places = [pl.ds(pl.multiple_of(codes_ref[m, j], 2), 2) for j in range(16)]
-            sums = [t[places[j]] + values[pl.ds(m * 32 + j * 2, 2)] for j in range(16)]
+        pair = ((t0, i * 2), (t1, i * 2 + 1))
+        places = [[pl.ds(pl.multiple_of(codes_ref[j, m], 2), 2) for j in range(16)] for _, m in pair]
+        sums = [
+            [t[places[n][j]] + values[pl.ds(m * 32 + j * 2, 2)] for j in range(16)] for n, (t, m) in enumerate(pair)
+        ]
+        for n, (t, m) in enumerate(pair):
             for j in range(16):
-                t[places[j]] = sums[j]
+                t[places[n][j]] = sums[n][j]
         return carry
 
     lax.fori_loop(0, 64, add_messages, 0)
@@ -528,14 +621,14 @@
         out_specs=(hbm, hbm),
         scratch_shapes=[
             pltpu.VMEM((2048, 128), jnp.int32),
-            pltpu.SMEM((128, 128), jnp.int32),
-            pltpu.VMEM((128, 128), jnp.int32),
+            pltpu.SMEM((16, 128), jnp.int32),
+            pltpu.VMEM((16, 128), jnp.int32),
             pltpu.VMEM((256, 256), jnp.float32),
-            pltpu.VMEM((4096, 128), jnp.float32),
-            pltpu.VMEM((2 * ITEM_DEV + 16, 128), jnp.float32),
-            pltpu.VMEM((2 * ITEM_DEV + 16, 128), jnp.float32),
+            pltpu.VMEM((4104, 128), jnp.float32),
+            pltpu.VMEM((2 * ITEM_DEV + 32, 128), jnp.float32),
+            pltpu.VMEM((2 * ITEM_DEV + 32, 128), jnp.float32),
             pltpu.VMEM((ITEM_DEV, 256), jnp.float32),
-            pltpu.SemaphoreType.DMA((13,)),
+            pltpu.SemaphoreType.DMA((16,)),
         ],
         compiler_params=pltpu.CompilerParams(vmem_limit_bytes=64 * 1024 * 1024),
         cost_estimate=pl.CostEstimate(flops=2_000_000, bytes_accessed=5_500_000, transcendentals=0),
@@ -550,17 +643,16 @@
         out_shape=(
             jax.ShapeDtypeStruct((256, 256), jnp.float32),
             jax.ShapeDtypeStruct((128, 16, 128), jnp.int32),
-            jax.ShapeDtypeStruct((128, 1, 128), jnp.int32),
+            jax.ShapeDtypeStruct((32, 128), jnp.int32),
         ),
         in_specs=[pl.BlockSpec(memory_space=pltpu.HBM)] * 10,
-        out_specs=(vmem, pl.BlockSpec(memory_space=pl.ANY), pl.BlockSpec(memory_space=pl.ANY)),
+        out_specs=(vmem, pl.BlockSpec(memory_space=pl.ANY), vmem),
         scratch_shapes=[
             pltpu.VMEM((256, 256), jnp.bfloat16),
             pltpu.VMEM((1, 256), jnp.int32),
             pltpu.VMEM((1, 256), jnp.int32),
             pltpu.VMEM((16, 256), jnp.float32),
             pltpu.VMEM((1, 256), jnp.float32),
-            pltpu.VMEM((256, 256), jnp.bfloat16),
             pltpu.VMEM((256, 256), jnp.bfloat16),
             pltpu.VMEM((2, 512, 256), jnp.bfloat16),
             pltpu.VMEM((2, 512), jnp.int32),
@@ -569,7 +661,9 @@
             pltpu.VMEM((2, 512, 256), jnp.bfloat16),
             pltpu.VMEM((256, 256), jnp.float32),
             pltpu.VMEM((16, 2, 136, 128), jnp.int32),
-            pltpu.VMEM((2, 3, 4, 136, 128), jnp.int32),
+            pltpu.VMEM((2, 2, 4, 136, 128), jnp.int32),
+            pltpu.VMEM((2, 4, 136, 128), jnp.int32),
+            pltpu.VMEM((2, 4, 136, 128), jnp.int32),
             pltpu.VMEM((2, 3, 136, 128), jnp.int32),
             pltpu.VMEM((2, 3, 136, 128), jnp.int32),
             pltpu.VMEM((2, 512, 256), jnp.float32),
@@ -579,11 +673,16 @@
             pltpu.VMEM((1024, 512), jnp.bfloat16),
             pltpu.VMEM((128, 16, 128), jnp.int32),
             pltpu.VMEM((128, 1, 128), jnp.int32),
+            pltpu.VMEM((128, 1, 128), jnp.int32),
+            pltpu.VMEM((128, 1024), jnp.float32),
+            pltpu.VMEM((128, 1024), jnp.float32),
             pltpu.SemaphoreType.DMA((10,)),
             pltpu.SemaphoreType.DMA((len(SENDS),)),
             pltpu.SemaphoreType.DMA((16, 4)),
             pltpu.SemaphoreType.DMA((16, 2)),
-            pltpu.SemaphoreType.DMA((2, 3, 4)),
+            pltpu.SemaphoreType.DMA((2, 2, 4)),
+            pltpu.SemaphoreType.DMA((2, 4)),
+            pltpu.SemaphoreType.DMA((2, 4)),
             pltpu.SemaphoreType.DMA((2, 3)),
             pltpu.SemaphoreType.DMA((2, 3)),
             pltpu.SemaphoreType.DMA,
@@ -621,7 +720,7 @@
         candidates, scenarios, candidate_user, gate_table, log_normalizer,
         forward_out, out_grad, history, history_items, history_length,
     )
-    table_grad, candidate_grad = add_rows(rows.reshape(2048, 128), codes.reshape(128, 128), candidate_grad)
+    table_grad, candidate_grad = add_rows(rows.reshape(2048, 128), codes, candidate_grad)
     return (candidate_grad, table_grad)
 
 

time: 71 us -> 69.7 us (0.982)
  Pallas kernels: 69.8 us -> 68.9 us
    pallas_call x1, Pallas kernels: 62.4 us -> 61.7 us  [attention(): pl.pallas_call(attention_kernel, out_shape=(jax.ShapeDtypeStruct((256, 25...]
where the time goes in v1:
time: 69.7 us; the launch traced here: 69.5 us
  Pallas kernels  68.9 us (99%)
    pallas_call x1, Pallas kernels, attention(): pl.pallas_call(attention_kernel, out_shape=(jax.ShapeDtypeStruct((256, 25...  61.7 us
    pallas_call x1, Pallas kernels, add_rows(): pl.pallas_call(table_kernel, out_shape=(jax.ShapeDtypeStruct((ITEM_DEV, 2...  7.23 us

profile of v1, /device:TPU:0, one launch (start us, length us, event | category | flops | bytes accessed | tf_op | source)
XLA Modules:
  0.0 69.5 jit_solution(13927066159831380855)
XLA Ops:
  0.6 61.7 %attention_grads.1 = (f32[256,256]{1,0:T(8,128)}, s32[128,16,128]{2,1,0:T(8,128)}, s32[32,128]{1,0:T(8,128)}) custom-call(bf16[256,256]{1,0:T(8,128)(2,1)} %cand_hbm.1, s32[1,256]{1,0:T(1,128)} %bitcast.5, s32[1,256]{1,0:T(1,128)} %bitcast.6, f32[16,256]{1,0:T(8,128)} %gate_hbm.1, f32[1,256]{1,0:T(1,128)} %bitcast.7, bf16[256,256]{1,0:T(8,128)(2,1)} %fwd_hbm.1, ...), custom_call_target="tpu_custom_call" | custom-call | flops 5400000000 | bytes 4000000 | tf_op jit(solution)/shard_map/attention_grads/pallas_call | solution.py:641
  62.3 7.2 %table_rows.1 = (f32[4096,256]{1,0:T(8,128)}, f32[256,256]{1,0:T(8,128)}) custom-call(s32[2048,128]{1,0:T(8,128)} %bitcast.4, s32[32,128]{1,0:T(8,128)} %get-tuple-element.8.codes_hbm, f32[256,256]{1,0:T(8,128)} %get-tuple-element.9.cand_hbm), custom_call_target="tpu_custom_call" | custom-call | flops 2000000 | bytes 5500000 | tf_op jit(solution)/shard_map/table_rows/pallas_call | solution.py:614

commit v2 on v1

--- a/solution.py
+++ b/solution.py
@@ -477,11 +477,12 @@
                 send_one()
         return carry
 
+    lax.fori_loop(0, 2, send_chunk, 0)
     for across in (0, 1, 3, 2):
         for h in range(2):
             pass_on(h, across)
 
-    lax.fori_loop(0, 8, send_chunk, 0)
+    lax.fori_loop(2, 8, send_chunk, 0)
     own_rows.start()
     own_codes.start()
 

time: 69.7 us -> 68.1 us (0.977)
  the two profiles are of different devices: /device:TPU:0 before, /device:TPU:24 now
where the time goes in v2:
time: 68.1 us; the launch traced here: 67.9 us
  Pallas kernels  67.3 us (99%)
    pallas_call x1, Pallas kernels, attention(): pl.pallas_call(attention_kernel, out_shape=(jax.ShapeDtypeStruct((256, 25...  60 us
    pallas_call x1, Pallas kernels, add_rows(): pl.pallas_call(table_kernel, out_shape=(jax.ShapeDtypeStruct((ITEM_DEV, 2...  7.23 us

profile of v2, /device:TPU:24, one launch (start us, length us, event | category | flops | bytes accessed | tf_op | source)
XLA Modules:
  0.0 67.9 jit_solution(12601514283870686608)
XLA Ops:
  0.6 60.0 %attention_grads.1 = (f32[256,256]{1,0:T(8,128)}, s32[128,16,128]{2,1,0:T(8,128)}, s32[32,128]{1,0:T(8,128)}) custom-call(bf16[256,256]{1,0:T(8,128)(2,1)} %cand_hbm.1, s32[1,256]{1,0:T(1,128)} %bitcast.5, s32[1,256]{1,0:T(1,128)} %bitcast.6, f32[16,256]{1,0:T(8,128)} %gate_hbm.1, f32[1,256]{1,0:T(1,128)} %bitcast.7, bf16[256,256]{1,0:T(8,128)(2,1)} %fwd_hbm.1, ...), custom_call_target="tpu_custom_call" | custom-call | flops 5400000000 | bytes 4000000 | tf_op jit(solution)/shard_map/attention_grads/pallas_call | solution.py:642
  60.7 7.2 %table_rows.1 = (f32[4096,256]{1,0:T(8,128)}, f32[256,256]{1,0:T(8,128)}) custom-call(s32[2048,128]{1,0:T(8,128)} %bitcast.4, s32[32,128]{1,0:T(8,128)} %get-tuple-element.8.codes_hbm, f32[256,256]{1,0:T(8,128)} %get-tuple-element.9.cand_hbm), custom_call_target="tpu_custom_call" | custom-call | flops 2000000 | bytes 5500000 | tf_op jit(solution)/shard_map/table_rows/pallas_call | solution.py:615

commit v3 on v1

--- a/solution.py
+++ b/solution.py
@@ -477,11 +477,17 @@
                 send_one()
         return carry
 
-    for across in (0, 1, 3, 2):
+    lax.fori_loop(0, 1, send_chunk, 0)
+    for across in (0, 1):
         for h in range(2):
             pass_on(h, across)
 
-    lax.fori_loop(0, 8, send_chunk, 0)
+    lax.fori_loop(1, 3, send_chunk, 0)
+    for across in (3, 2):
+        for h in range(2):
+            pass_on(h, across)
+
+    lax.fori_loop(3, 8, send_chunk, 0)
     own_rows.start()
     own_codes.start()
 

time: 69.7 us -> 68 us (0.976)
  Pallas kernels: 68.9 us -> 67.2 us
    pallas_call x1, Pallas kernels: 61.7 us -> 60 us  [attention(): pl.pallas_call(attention_kernel, out_shape=(jax.ShapeDtypeStruct((256, 25...]
where the time goes in v3:
time: 68 us; the launch traced here: 67.9 us
  Pallas kernels  67.2 us (99%)
    pallas_call x1, Pallas kernels, attention(): pl.pallas_call(attention_kernel, out_shape=(jax.ShapeDtypeStruct((256, 25...  60 us
    pallas_call x1, Pallas kernels, add_rows(): pl.pallas_call(table_kernel, out_shape=(jax.ShapeDtypeStruct((ITEM_DEV, 2...  7.23 us

profile of v3, /device:TPU:0, one launch (start us, length us, event | category | flops | bytes accessed | tf_op | source)
XLA Modules:
  0.0 67.9 jit_solution(4531382380906888548)
XLA Ops:
  0.6 60.0 %attention_grads.1 = (f32[256,256]{1,0:T(8,128)}, s32[128,16,128]{2,1,0:T(8,128)}, s32[32,128]{1,0:T(8,128)}) custom-call(bf16[256,256]{1,0:T(8,128)(2,1)} %cand_hbm.1, s32[1,256]{1,0:T(1,128)} %bitcast.5, s32[1,256]{1,0:T(1,128)} %bitcast.6, f32[16,256]{1,0:T(8,128)} %gate_hbm.1, f32[1,256]{1,0:T(1,128)} %bitcast.7, bf16[256,256]{1,0:T(8,128)(2,1)} %fwd_hbm.1, ...), custom_call_target="tpu_custom_call" | custom-call | flops 5400000000 | bytes 4000000 | tf_op jit(solution)/shard_map/attention_grads/pallas_call | solution.py:647
  60.6 7.2 %table_rows.1 = (f32[4096,256]{1,0:T(8,128)}, f32[256,256]{1,0:T(8,128)}) custom-call(s32[2048,128]{1,0:T(8,128)} %bitcast.4, s32[32,128]{1,0:T(8,128)} %get-tuple-element.8.codes_hbm, f32[256,256]{1,0:T(8,128)} %get-tuple-element.9.cand_hbm), custom_call_target="tpu_custom_call" | custom-call | flops 2000000 | bytes 5500000 | tf_op jit(solution)/shard_map/table_rows/pallas_call | solution.py:620
